TPU v7x, 512 devices: a whole 4x4x16 slice. The times are simulated.
512 devices in a mesh: design: 16 (over y, x_lo, core), seq: 32 (over x_hi, z).
Axes of the slice: x: 4 (x_hi: 2, x_lo: 2; x = x_hi * 2 + x_lo), y: 4, z: 16, core: 2. Of those that a mesh axis runs over, the one named last changes fastest.
Arguments:
- window_x: bfloat16 [16, 512, 8192], P('design', 'seq'), may hold values from -6 to 6
- norm_gain: float32 [8192], replicated, may hold values from 0.5 to 1.5
- proj_weight: bfloat16 [8192, 3, 4096], P('design', None, 'seq'), may hold values from -0.0625 to 0.0625
- proj_tail: bfloat16 [16, 6, 3, 4096], P('design', None, None, 'seq'), may hold values from -6 to 6
- short_taps: float32 [7, 3, 4096], P(None, None, 'seq'), may hold values from -2 to 2
- decay_rates: float32 [4096, 16], replicated, may hold values from 8.680556e-06 to 0.035
- residues: float32 [4096, 16], P('seq'), may hold values from 0 to 0.03
- skip_bias: float32 [4096], P('seq'), may hold values from -6 to 6
- context_u: bfloat16 [16, 4096, 4096], P('design', 'seq'), may hold values from -6 to 6
- context_tokens: int32 [16, 4096], P('design', 'seq'), may hold values from 0 to 4, as said below
Outputs:
- mixed: bfloat16 [16, 512, 4096], P('design', None, 'seq')
Inputs may be any that keep to these rules, and one draw needn't show every extreme that they name: `context_tokens`: 0 marks padding and fills a prefix of 1 to 65 positions of each design's context; 1 to 4 are bases.
All inputs are finite; a program needn't handle non-finite values.
Results may differ from a plain program's by a relative error of at most 0.0059.
The roundings to bfloat16 on the way count: a program that leaves them out, or rounds other values in their place, can miss the bound.
Values may be sent and summed in bfloat16 or wider, within the bound.
No kernel may reach another device: no remote copies, remote signals or barrier semaphores. Data moves between devices by JAX's collectives and lax.ppermute only.
A program may use at most 128 MiB of HBM per device.

v0:
```python
import math
import jax
import jax.numpy as jnp
from jax import lax
from jax.sharding import PartitionSpec as P


def decayed_sum(values, distance, rate_table):
    columns = []
    for mode_index in range(rate_table.shape[1]):
        weights = jnp.exp(-rate_table[:, mode_index][None, :] * distance[:, None])
        columns.append(jnp.sum(values * weights, axis=0))
    return jnp.stack(columns, axis=1)


def dft_tables(length):
    indices = jnp.arange(length, dtype=jnp.int32)
    phase_int = indices[:, None] * indices[None, :] % length
    angles = phase_int.astype(jnp.float32) * (2.0 * math.pi / length)
    return (jnp.cos(angles), jnp.sin(angles))


def local(
    window_x,
    norm_gain,
    proj_weight,
    proj_tail,
    short_taps,
    decay_rates,
    residues,
    skip_bias,
    context_u,
    context_tokens,
):
    local_rows = window_x.shape[1]
    width = window_x.shape[2]
    local_chans = proj_weight.shape[2]
    seq_count = lax.axis_size("seq")
    window = local_rows * seq_count
    ctx_rows = context_u.shape[1]
    history = ctx_rows * seq_count
    seq_index = lax.axis_index("seq")
    highest = lax.Precision.HIGHEST
    rows_f = window_x[0].astype(jnp.float32)
    meansq = jnp.mean(rows_f * rows_f, axis=-1, keepdims=True)
    normed = (rows_f * lax.rsqrt(meansq + 1e-06) * norm_gain[None, :]).astype(jnp.bfloat16)
    weight_panel = lax.all_gather(proj_weight, "design", axis=0, tiled=True).reshape(
        width, 3 * local_chans
    )
    features = jnp.dot(
        lax.all_gather(normed, "seq", axis=0, tiled=True),
        weight_panel,
        preferred_element_type=jnp.float32,
    )
    features = features.astype(jnp.bfloat16).reshape(window, 3, local_chans)
    extended = jnp.concatenate([proj_tail[0], features], axis=0).astype(jnp.float32)
    filtered = jnp.zeros((window, 3, local_chans), jnp.float32)
    for tap_index in range(short_taps.shape[0]):
        begin_row = short_taps.shape[0] - 1 - tap_index
        filtered = filtered + short_taps[tap_index][None] * extended[begin_row : begin_row + window]
    queries = filtered[:, 0]
    inner_term = filtered[:, 1] * filtered[:, 2]
    rates_local = lax.dynamic_slice_in_dim(decay_rates, seq_index * local_chans, local_chans, 0)
    masked_hist = jnp.where(
        (context_tokens[0] != 0)[:, None], context_u[0], jnp.zeros((), jnp.bfloat16)
    )
    relaid = lax.all_to_all(masked_hist, "seq", split_axis=1, concat_axis=0, tiled=True)
    distance = (history - 1 - jnp.arange(history, dtype=jnp.int32)).astype(jnp.float32)
    states = decayed_sum(relaid.astype(jnp.float32), distance, rates_local)
    offsets = jnp.arange(window, dtype=jnp.int32).astype(jnp.float32)
    decay_grid = jnp.exp(-rates_local[None, :, :] * offsets[:, None, None])
    kernel = jnp.einsum("tcm,cm->tc", decay_grid, residues, precision=highest)
    carried = jnp.einsum(
        "tcm,cm->tc", decay_grid, residues * jnp.exp(-rates_local) * states, precision=highest
    )
    length = 2 * window
    cos_table, sin_table = dft_tables(length)
    zero_rows = jnp.zeros((window, local_chans), jnp.float32)

    def spectrum(values):
        padded = jnp.concatenate([values, zero_rows], axis=0)
        real_part = jnp.dot(cos_table, padded, precision=highest)
        imag_part = -jnp.dot(sin_table, padded, precision=highest)
        return (real_part, imag_part)

    inner_re, inner_im = spectrum(inner_term)
    kernel_re, kernel_im = spectrum(kernel)
    prod_re = inner_re * kernel_re - inner_im * kernel_im
    prod_im = inner_re * kernel_im + inner_im * kernel_re
    longconv = (
        jnp.dot(cos_table[:window], prod_re, precision=highest)
        - jnp.dot(sin_table[:window], prod_im, precision=highest)
    ) / length
    output_block = (queries * (longconv + carried + skip_bias[None, :] * inner_term)).astype(
        jnp.bfloat16
    )
    return output_block[None]


def solution(mesh):
    in_specs = (
        P("design", "seq", None),
        P(),
        P("design", None, "seq"),
        P("design", None, None, "seq"),
        P(None, None, "seq"),
        P(),
        P("seq", None),
        P("seq"),
        P("design", "seq", None),
        P("design", "seq"),
    )
    out_specs = P("design", None, "seq")
    return jax.shard_map(local, mesh=mesh, in_specs=in_specs, out_specs=out_specs, check_vma=False)
```

profile of v0, /device:TPU:32, one launch (start us, length us, event | category | flops | bytes accessed | tf_op | source)
XLA Modules:
  0.0 330.9 jit_solution(15777754056590807734)
XLA Ops:
  6.5 0.0 copy-start.6
  6.5 0.0 all-gather.5.cloned.1.call-start
  6.5 1.9 copy.29
  8.5 0.0 all-gather.5.cloned.1.call-update
  8.5 0.0 all-gather.3.cloned.1.call-start
  8.5 1.1 fusion.67
  9.7 1.8 fusion.69
  11.5 0.0 all-gather.3.cloned.1.call-update
  11.5 0.0 copy-start.4
  11.5 0.0 copy-start.2
  11.5 1.6 copy.31
  13.1 0.0 copy-done.6
  13.2 0.1 broadcast_select_fusion
  13.2 1.3 copy.32
  14.6 17.8 %all-to-all-start = ((bf16[128,32,128]{2,0,1:T(8,128)(2,1)}), bf16[128,32,128]{2,0,1:T(8,128)(2,1)S(1)}, u32[]{:S(2)}, u32[]{:S(2)}) async-start(bf16[128,32,128]{2,0,1:T(8,128)(2,1)} %copy.32), calls=%async_computation | async-start | bytes 2097152 | tf_op jit(solution)/shard_map/all_to_all | solution.py:67
  32.4 0.0 copy-done.4
  32.4 0.0 copy-done.2
  32.5 1.1 fusion.94
  33.7 16.2 %fusion.27 = f32[1024,1024]{1,0:T(8,128)} fusion(), kind=kLoop, calls=%fused_computation.49 | loop fusion | flops 14680064 | bytes 4194304 | tf_op jit(solution)/shard_map/cos | solution.py:20
  49.9 16.3 %fusion.26 = f32[1024,1024]{1,0:T(8,128)} fusion(), kind=kLoop, calls=%fused_computation.48 | loop fusion | flops 14680064 | bytes 4194304 | tf_op jit(solution)/shard_map/sin | solution.py:20
  66.2 22.2 %all-to-all-done = bf16[128,32,128]{2,0,1:T(8,128)(2,1)S(1)} async-done(((bf16[128,32,128]{2,0,1:T(8,128)(2,1)}), bf16[128,32,128]{2,0,1:T(8,128)(2,1)S(1)}, u32[]{:S(2)}, u32[]{:S(2)}) %all-to-all-start) | async-done | bytes 1048608 | tf_op jit(solution)/shard_map/all_to_all | solution.py:67
  88.4 0.0 copy-start.3
  88.4 5.9 %fusion.25 = (f32[128]{0:T(128)S(1)}, f32[128]{0:T(128)S(1)}, f32[128]{0:T(128)S(1)}, f32[128]{0:T(128)S(1)}, f32[128]{0:T(128)S(1)}, /*index=5*/f32[128]{0:T(12...) fusion(bf16[128,32,128]{2,0,1:T(8,128)(2,1)S(1)} %all-to-all-do, ...), kind=kLoop, calls=%fused_computation.47 | loop fusion | flops 25688064 | bytes 1081344 | tf_op jit(solution)/shard_map/reduce_sum | solution.py:12
  94.2 0.1 stack.67
  94.3 0.0 copy-done.3
  94.3 0.7 multiply_multiply_fusion
  95.0 3.1 multiply_reduce_fusion
  98.1 0.1 copy.38
  98.2 18.9 %fusion.32 = f32[1024,128]{1,0:T(8,128)S(1)} fusion(f32[512,128]{0,1:T(8,128)S(1)} %bitcast.143), kind=kOutput, calls=%fused_computation.52 | convolution fusion | flops 1625292800 | bytes 786432 | tf_op jit(solution)/shard_map/dot_general | solution.py:83
  117.2 19.2 %fusion.28 = f32[1024,128]{1,0:T(8,128)S(1)} fusion(f32[512,128]{0,1:T(8,128)S(1)} %bitcast.144), kind=kOutput, calls=%fused_computation.50 | convolution fusion | flops 1625292800 | bytes 786432 | tf_op jit(solution)/shard_map/dot_general | solution.py:82
  136.3 0.0 all-gather.5.cloned.1.call-done
  136.3 135.1 %all-gather.3.cloned.1.call-done = bf16[512,8192]{1,0:T(8,128)(2,1)} async-done(((bf16[16,8192]{1,0:T(8,128)(2,1)}), bf16[512,8192]{1,0:T(8,128)(2,1)}) %all-gather.3.cloned.1.call-update) | async-done | bytes 8388624 | tf_op jit(solution)/shard_map/all_gather | solution.py:51
  271.4 8.6 %convolution_convert_fusion = bf16[512,384]{0,1:T(8,128)(2,1)S(1)} fusion(bf16[512,8192]{1,0:T(8,128)(2,1)} %all-gather.3.cloned.1.call-done, bf16[8192,384]{0,1:T(8,128)(2,1)} %bitcast.163), kind=kOutput, calls=%fused_computation.54 | convolution fusion | flops 3221422080 | bytes 15073280 | tf_op jit(solution)/shard_map/dot_general | solution.py:50
  280.0 0.2 copy.30
  280.2 0.1 maximum_convert_fusion
  280.3 0.6 fusion.57
  281.0 19.4 %fusion.34 = f32[1024,128]{1,0:T(8,128)S(1)} fusion(f32[512,128]{1,0:T(8,128)S(1)} %fusion.78), kind=kOutput, calls=%fused_computation.53 | convolution fusion | flops 1625292800 | bytes 786432 | tf_op jit(solution)/shard_map/dot_general | solution.py:83
  300.4 0.0 copy-start.1
  300.4 18.8 %fusion.30 = f32[1024,128]{1,0:T(8,128)S(1)} fusion(f32[512,128]{1,0:T(8,128)S(1)} %fusion.78), kind=kOutput, calls=%fused_computation.51 | convolution fusion | flops 1625292800 | bytes 786432 | tf_op jit(solution)/shard_map/dot_general | solution.py:82
  319.2 0.0 copy-done.1
  319.2 0.0 copy-start
  319.2 0.0 copy-start.5
  319.2 1.8 fusion.6
  321.0 0.3 copy-done
  321.4 0.0 copy-done.5
  321.4 2.5 fusion.54
  (11 shorter events, 0.1 us)
Async XLA Ops:
  6.5 6.6 %copy-start.6 = (s32[1,128]{1,0:T(1,128)S(1)}, s32[1,128]{1,0:T(1,128)}, u32[]{:S(2)}) copy-start(s32[1,128]{1,0:T(1,128)} %param.19) | copy-start | bytes 1540
  6.5 129.8 %all-gather.5.cloned.1.call-start = ((), (), s32[]{:S(2)}) async-start(), calls=%async_computation.2 | async-start | bytes 6684672 | tf_op jit(solution)/shard_map/all_gather | solution.py:47
  8.5 262.9 %all-gather.3.cloned.1.call-start = ((), (), s32[]{:S(2)}) async-start(), calls=%async_computation.1 | async-start | bytes 8650752 | tf_op jit(solution)/shard_map/all_gather | solution.py:51
  11.5 20.9 %copy-start.4 = (bf16[1,6,3,128]{3,2,1,0:T(4,128)(2,1)S(1)}, bf16[1,6,3,128]{3,2,1,0:T(4,128)(2,1)}, u32[]{:S(2)}) copy-start(bf16[1,6,3,128]{3,2,1,0:T(4,128)(2,1)} %param.13) | copy-start | bytes 13828
  11.5 20.9 %copy-start.2 = (f32[7,3,128]{2,0,1:T(8,128)S(1)}, f32[7,3,128]{2,0,1:T(8,128)}, u32[]{:S(2)}) copy-start(f32[7,3,128]{2,0,1:T(8,128)} %param.14) | copy-start | bytes 32260
  14.6 73.8 %all-to-all-start = ((bf16[128,32,128]{2,0,1:T(8,128)(2,1)}), bf16[128,32,128]{2,0,1:T(8,128)(2,1)S(1)}, u32[]{:S(2)}, u32[]{:S(2)}) async-start(bf16[128,32,128]{2,0,1:T(8,128)(2,1)} %copy.32), calls=%async_computation | async-start | bytes 2097152 | tf_op jit(solution)/shard_map/all_to_all | solution.py:67
  88.4 5.9 %copy-start.3 = (f32[128,16]{0,1:T(8,128)S(1)}, f32[128,16]{0,1:T(8,128)}, u32[]{:S(2)}) copy-start(f32[128,16]{0,1:T(8,128)} %param.16) | copy-start | bytes 24580
  300.4 18.8 %copy-start.1 = (f32[1024,1024]{1,0:T(8,128)S(1)}, f32[1024,1024]{1,0:T(8,128)}, u32[]{:S(2)}) copy-start(f32[1024,1024]{1,0:T(8,128)} %fusion.26) | copy-start | bytes 12582916
  319.2 2.2 copy-start
  319.2 2.2 copy-start.5
Sparse Core Ops, SparseCore 0:
  9.5 62.8 all-gather.4
  75.4 195.9 all-gather.2
where the time goes:
time: 337 us; the launch traced here: 331 us
  waiting for transfers between devices  157 us (47%)
  matrix products  89.1 us (26%)
  other arithmetic  47.1 us (14%)
  starting transfers between devices  17.9 us (5%)
  between operations  13.9 us (4%)
  local copies, waits for them, and re-layouts  5.67 us (2%)
    all_gather x1, waiting for transfers between devices, local(): lax.all_gather(normed, 'seq', axis=0, tiled=True)  135 us
    dot_general x2, matrix products, spectrum(): imag_part = -jnp.dot(sin_table, padded, precision=highest)  38.3 us
    dot_general x2, matrix products, spectrum(): real_part = jnp.dot(cos_table, padded, precision=highest)  37.9 us
    all_to_all x1, waiting for transfers between devices, local(): lax.all_to_all(masked_hist, 'seq', split_axis=1, concat_axis=0, tiled=True)  22.2 us
    all_to_all x1, starting transfers between devices, local(): lax.all_to_all(masked_hist, 'seq', split_axis=1, concat_axis=0, tiled=True)  17.8 us
    sin x1, other arithmetic, dft_tables(): return (jnp.cos(angles), jnp.sin(angles))  16.3 us
    cos x1, other arithmetic, dft_tables(): return (jnp.cos(angles), jnp.sin(angles))  16.2 us
    dot_general x1, matrix products, local(): jnp.dot(lax.all_gather(normed, 'seq', axis=0, tiled=True), weight_panel,...  8.6 us
  transfers between devices with their start and end apart: 3, of which 2 were waited for; matrix products, arithmetic and copies ran while one was open for 26% of the time, Pallas kernels for 0%

commit v1 on v0

--- a/solution.py
+++ b/solution.py
@@ -48,7 +48,9 @@
         width, 3 * local_chans
     )
     features = jnp.dot(
-        lax.all_gather(normed, "seq", axis=0, tiled=True),
+        jnp.concatenate(
+            lax.all_to_all(jnp.stack([normed] * lax.axis_size("seq")), "seq", 0, 0), axis=0
+        ),
         weight_panel,
         preferred_element_type=jnp.float32,
     )

time: 337 us -> 529 us (1.57)
  the two profiles are of different devices: /device:TPU:32 before, /device:TPU:120 now
where the time goes in v1:
time: 529 us; the launch traced here: 522 us
  waiting for transfers between devices  342 us (65%)
  matrix products  89.1 us (17%)
  other arithmetic  45.2 us (9%)
  starting transfers between devices  23.5 us (4%)
  between operations  13.9 us (3%)
  local copies, waits for them, and re-layouts  8.99 us (2%)
    all_to_all x1, waiting for transfers between devices, local(): lax.all_to_all(jnp.stack([normed] * lax.axis_size('seq')), 'seq', 0, 0)  288 us
    all_to_all x1, waiting for transfers between devices, local(): lax.all_to_all(masked_hist, 'seq', split_axis=1, concat_axis=0, tiled=True)  53.6 us
    dot_general x2, matrix products, spectrum(): imag_part = -jnp.dot(sin_table, padded, precision=highest)  38.1 us
    dot_general x2, matrix products, spectrum(): real_part = jnp.dot(cos_table, padded, precision=highest)  38.1 us
    all_to_all x1, starting transfers between devices, local(): lax.all_to_all(masked_hist, 'seq', split_axis=1, concat_axis=0, tiled=True)  16.9 us
    sin x1, other arithmetic, dft_tables(): return (jnp.cos(angles), jnp.sin(angles))  16.3 us
    cos x1, other arithmetic, dft_tables(): return (jnp.cos(angles), jnp.sin(angles))  16.2 us
  transfers between devices with their start and end apart: 3, of which 2 were waited for; matrix products, arithmetic and copies ran while one was open for 16% of the time, Pallas kernels for 0%

profile of v1, /device:TPU:120, one launch (start us, length us, event | category | flops | bytes accessed | tf_op | source)
XLA Modules:
  0.0 522.3 jit_solution(7101642024298922101)
XLA Ops:
  6.5 0.0 copy-start.2
  6.5 0.0 copy-start.4
  6.5 1.7 copy.31
  8.2 0.7 compare_bitcast_fusion
  8.9 0.1 broadcast_select_fusion
  8.9 1.3 copy.32
  10.3 16.9 %all-to-all-start.1 = ((bf16[128,32,128]{2,0,1:T(8,128)(2,1)}), bf16[128,32,128]{2,0,1:T(8,128)(2,1)S(1)}, u32[]{:S(2)}, u32[]{:S(2)}) async-start(bf16[128,32,128]{2,0,1:T(8,128)(2,1)} %copy.32), calls=%async_computation.1 | async-start | bytes 2097152 | tf_op jit(solution)/shard_map/all_to_all | solution.py:69
  27.2 0.0 copy-done.2
  27.2 0.2 fusion.67
  27.4 0.0 copy-done.4
  27.4 0.1 fusion.78
  27.5 53.6 %all-to-all-done.1 = bf16[128,32,128]{2,0,1:T(8,128)(2,1)S(1)} async-done(((bf16[128,32,128]{2,0,1:T(8,128)(2,1)}), bf16[128,32,128]{2,0,1:T(8,128)(2,1)S(1)}, u32[]{:S(2)}, u32[]{:S(2)}) %all-to-all-start.1) | async-done | bytes 1048608 | tf_op jit(solution)/shard_map/all_to_all | solution.py:69
  81.2 4.2 stack.39
  85.4 0.0 copy-start.3
  85.4 6.6 %all-to-all-start = ((bf16[32,16,8192]{2,1,0:T(8,128)(2,1)}), bf16[32,16,8192]{2,1,0:T(8,128)(2,1)}, u32[]{:S(2)}, u32[]{:S(2)}) async-start(bf16[32,16,8192]{2,1,0:T(8,128)(2,1)} %stack.39), calls=%async_computation | async-start | bytes 16777216 | tf_op jit(solution)/shard_map/all_to_all | solution.py:52
  92.0 0.0 all-gather.2.cloned.1.call-start
  92.0 0.0 copy-done.3
  92.0 1.0 copy.29
  93.0 0.0 all-gather.2.cloned.1.call-update
  93.0 0.0 copy-done.5
  93.1 0.0 copy-done.7
  93.1 1.1 fusion.95
  94.3 16.3 %fusion.26 = f32[1024,1024]{1,0:T(8,128)} fusion(), kind=kLoop, calls=%fused_computation.48 | loop fusion | flops 14680064 | bytes 4194304 | tf_op jit(solution)/shard_map/sin | solution.py:20
  110.6 16.2 %fusion.27 = f32[1024,1024]{1,0:T(8,128)} fusion(), kind=kLoop, calls=%fused_computation.49 | loop fusion | flops 14680064 | bytes 4194304 | tf_op jit(solution)/shard_map/cos | solution.py:20
  126.9 5.9 %fusion.25 = (f32[128]{0:T(128)S(1)}, f32[128]{0:T(128)S(1)}, f32[128]{0:T(128)S(1)}, f32[128]{0:T(128)S(1)}, f32[128]{0:T(128)S(1)}, /*index=5*/f32[128]{0:T(12...) fusion(bf16[128,32,128]{2,0,1:T(8,128)(2,1)S(1)} %all-to-all-do, ...), kind=kLoop, calls=%fused_computation.47 | loop fusion | flops 25688064 | bytes 1081344 | tf_op jit(solution)/shard_map/reduce_sum | solution.py:12
  132.7 0.1 stack.106
  132.8 0.0 copy-done.6
  132.8 0.7 multiply_multiply_fusion
  133.5 3.1 multiply_reduce_fusion
  136.6 0.1 copy.38
  136.8 18.8 %fusion.28 = f32[1024,128]{1,0:T(8,128)S(1)} fusion(f32[512,128]{0,1:T(8,128)S(1)} %bitcast.142), kind=kOutput, calls=%fused_computation.50 | convolution fusion | flops 1625292800 | bytes 786432 | tf_op jit(solution)/shard_map/dot_general | solution.py:84
  155.6 19.3 %fusion.32 = f32[1024,128]{1,0:T(8,128)S(1)} fusion(f32[512,128]{0,1:T(8,128)S(1)} %bitcast.143), kind=kOutput, calls=%fused_computation.52 | convolution fusion | flops 1625292800 | bytes 786432 | tf_op jit(solution)/shard_map/dot_general | solution.py:85
  174.8 0.0 all-gather.2.cloned.1.call-done
  174.9 287.9 %all-to-all-done = bf16[32,16,8192]{2,1,0:T(8,128)(2,1)} async-done(((bf16[32,16,8192]{2,1,0:T(8,128)(2,1)}), bf16[32,16,8192]{2,1,0:T(8,128)(2,1)}, u32[]{:S(2)}, u32[]{:S(2)}) %all-to-all-start) | async-done | bytes 8388640 | tf_op jit(solution)/shard_map/all_to_all | solution.py:52
  462.8 8.6 %convolution_convert_fusion = bf16[512,384]{0,1:T(8,128)(2,1)S(1)} fusion(bf16[512,8192]{1,0:T(8,128)(2,1)} %bitcast.4, bf16[8192,384]{0,1:T(8,128)(2,1)} %bitcast.162), kind=kOutput, calls=%fused_computation.54 | convolution fusion | flops 3221422080 | bytes 15073280 | tf_op jit(solution)/shard_map/dot_general | solution.py:50
  471.4 0.2 copy.30
  471.7 0.1 maximum_convert_fusion
  471.8 0.6 fusion.57
  472.4 19.3 %fusion.30 = f32[1024,128]{1,0:T(8,128)S(1)} fusion(f32[512,128]{1,0:T(8,128)S(1)} %fusion.79), kind=kOutput, calls=%fused_computation.51 | convolution fusion | flops 1625292800 | bytes 786432 | tf_op jit(solution)/shard_map/dot_general | solution.py:84
  491.7 0.0 copy-start.1
  491.7 18.9 %fusion.34 = f32[1024,128]{1,0:T(8,128)S(1)} fusion(f32[512,128]{1,0:T(8,128)S(1)} %fusion.79), kind=kOutput, calls=%fused_computation.53 | convolution fusion | flops 1625292800 | bytes 786432 | tf_op jit(solution)/shard_map/dot_general | solution.py:85
  510.6 0.0 copy-done.1
  510.6 0.0 copy-start
  510.6 0.0 copy-start.8
  510.6 1.8 fusion.6
  512.4 0.3 copy-done
  512.8 0.0 copy-done.8
  512.8 2.5 fusion.54
  (13 shorter events, 0.1 us)
Async XLA Ops:
  6.5 20.6 %copy-start.2 = (bf16[1,16,8192]{2,1,0:T(8,128)(2,1)S(1)}, bf16[1,16,8192]{2,1,0:T(8,128)(2,1)}, u32[]{:S(2)}) copy-start(bf16[1,16,8192]{2,1,0:T(8,128)(2,1)} %param.10) | copy-start | bytes 786436
  6.5 20.9 %copy-start.4 = (f32[8192]{0:T(1024)S(1)}, f32[8192]{0:T(1024)}, u32[]{:S(2)}) copy-start(f32[8192]{0:T(1024)} %param.11) | copy-start | bytes 98308
  10.3 70.9 %all-to-all-start.1 = ((bf16[128,32,128]{2,0,1:T(8,128)(2,1)}), bf16[128,32,128]{2,0,1:T(8,128)(2,1)S(1)}, u32[]{:S(2)}, u32[]{:S(2)}) async-start(bf16[128,32,128]{2,0,1:T(8,128)(2,1)} %copy.32), calls=%async_computation.1 | async-start | bytes 2097152 | tf_op jit(solution)/shard_map/all_to_all | solution.py:69
  85.4 6.7 %copy-start.3 = (bf16[512,3,128]{2,0,1:T(8,128)(2,1)S(1)}, bf16[512,3,128]{2,0,1:T(8,128)(2,1)}, u32[]{:S(2)}) copy-start(bf16[512,3,128]{2,0,1:T(8,128)(2,1)} %param.12) | copy-start | bytes 1179652
  85.4 7.7 %copy-start.5 = (f32[7,3,128]{2,0,1:T(8,128)S(1)}, f32[7,3,128]{2,0,1:T(8,128)}, u32[]{:S(2)}) copy-start(f32[7,3,128]{2,0,1:T(8,128)} %param.14) | copy-start | bytes 32260
  85.4 7.7 %copy-start.7 = (bf16[1,6,3,128]{3,2,1,0:T(4,128)(2,1)S(1)}, bf16[1,6,3,128]{3,2,1,0:T(4,128)(2,1)}, u32[]{:S(2)}) copy-start(bf16[1,6,3,128]{3,2,1,0:T(4,128)(2,1)} %param.13) | copy-start | bytes 13828
  85.4 377.4 %all-to-all-start = ((bf16[32,16,8192]{2,1,0:T(8,128)(2,1)}), bf16[32,16,8192]{2,1,0:T(8,128)(2,1)}, u32[]{:S(2)}, u32[]{:S(2)}) async-start(bf16[32,16,8192]{2,1,0:T(8,128)(2,1)} %stack.39), calls=%async_computation | async-start | bytes 16777216 | tf_op jit(solution)/shard_map/all_to_all | solution.py:52
  92.0 82.9 %all-gather.2.cloned.1.call-start = ((), (), s32[]{:S(2)}) async-start(), calls=%async_computation.2 | async-start | bytes 6684672 | tf_op jit(solution)/shard_map/all_gather | solution.py:47
  126.9 5.9 %copy-start.6 = (f32[128,16]{0,1:T(8,128)S(1)}, f32[128,16]{0,1:T(8,128)}, u32[]{:S(2)}) copy-start(f32[128,16]{0,1:T(8,128)} %param.16) | copy-start | bytes 24580
  491.7 18.9 %copy-start.1 = (f32[1024,1024]{1,0:T(8,128)S(1)}, f32[1024,1024]{1,0:T(8,128)}, u32[]{:S(2)}) copy-start(f32[1024,1024]{1,0:T(8,128)} %fusion.26) | copy-start | bytes 12582916
  510.6 2.2 copy-start
  510.6 2.2 copy-start.8
Sparse Core Ops, SparseCore 0:
  94.9 62.0 all-gather.1
